TPU v7x, 512 devices: a whole 4x4x16 slice. The times are simulated.
512 devices in a mesh: dp: 32 (over z_lo, y, core), ctx: 16 (over x, z_hi).
Axes of the slice: x: 4, y: 4, z: 16 (z_hi: 4, z_lo: 4; z = z_hi * 4 + z_lo), core: 2. Of those that a mesh axis runs over, the one named last changes fastest.
Arguments:
- queries: bfloat16 [32, 128, 2560], P('dp', 'ctx'), may hold values from -5.5 to 5.5
- query_tangent: bfloat16 [32, 128, 2560], P('dp', 'ctx'), may hold values from -6 to 6
- keys: bfloat16 [32, 2304, 2560], P('dp', 'ctx'), may hold values from -5.5 to 5.5
- values: bfloat16 [32, 2304, 2560], P('dp', 'ctx'), may hold values from -6 to 6
- key_tangent: bfloat16 [32, 2304, 2560], P('dp', 'ctx'), may hold values from -6 to 6
- value_tangent: bfloat16 [32, 2304, 2560], P('dp', 'ctx'), may hold values from -6 to 6
- velocity: bfloat16 [32, 128, 2560], P('dp', 'ctx'), may hold values from -6 to 6
- out_weight: bfloat16 [2560, 2560], P('dp', 'ctx'), may hold values from -0.125 to 0.125
- pair_index: int32 [32, 2], P('dp'), may hold values from 0 to 14
Outputs:
- grad_queries: bfloat16 [32, 128, 2560], P('dp', 'ctx')
- grad_keys: bfloat16 [32, 2304, 2560], P('dp', 'ctx')
- grad_values: bfloat16 [32, 2304, 2560], P('dp', 'ctx')
All inputs are finite; a program needn't handle non-finite values.
Results may differ from a plain program's by a relative error of at most 0.029.
Values may be sent and summed in bfloat16 or wider, within the bound.
A program may use at most 64 MiB of HBM per device.

v0:
```python
import jax
import jax.numpy as jnp
from jax import lax
from jax.sharding import PartitionSpec as P

HEADS = 20
HDIM = 128


time_grid = 15.0


def local(
    queries,
    query_tangent,
    keys,
    values,
    key_tangent,
    value_tangent,
    velocity,
    out_weight,
    pair_index,
):
    scale = HDIM ** (-0.5)
    q_dev = queries.shape[1]
    kv_dev = keys.shape[1]
    width = queries.shape[2]
    n_ctx = lax.axis_size("ctx")
    rows = q_dev * n_ctx
    q_all, qt_all = (
        lax.all_gather(queries, "ctx", axis=1, tiled=True),
        lax.all_gather(query_tangent, "ctx", axis=1, tiled=True),
    )
    q_heads = q_all[0].reshape(rows, HEADS, HDIM)
    qt_heads = qt_all[0].reshape(rows, HEADS, HDIM)
    k_heads = keys[0].reshape(kv_dev, HEADS, HDIM)
    v_heads = values[0].reshape(kv_dev, HEADS, HDIM)
    kt_heads = key_tangent[0].reshape(kv_dev, HEADS, HDIM)
    vt_heads = value_tangent[0].reshape(kv_dev, HEADS, HDIM)
    score = jnp.einsum("qhd,khd->hqk", q_heads, k_heads, preferred_element_type=jnp.float32) * scale
    slope = (
        jnp.einsum("qhd,khd->hqk", qt_heads, k_heads, preferred_element_type=jnp.float32)
        + jnp.einsum("qhd,khd->hqk", q_heads, kt_heads, preferred_element_type=jnp.float32)
    ) * scale
    peak = jnp.max(score, axis=-1)
    expd = jnp.exp(score - peak[..., None])
    total = jnp.sum(expd, axis=-1)
    bend = jnp.sum(expd * slope, axis=-1)
    expd_b = expd.astype(jnp.bfloat16)
    mixed_b = (expd * slope).astype(jnp.bfloat16)
    part_a = jnp.einsum("hqk,khd->qhd", expd_b, v_heads, preferred_element_type=jnp.float32)
    part_c = jnp.einsum(
        "hqk,khd->qhd", mixed_b, v_heads, preferred_element_type=jnp.float32
    ) + jnp.einsum("hqk,khd->qhd", expd_b, vt_heads, preferred_element_type=jnp.float32)
    part_a = part_a.astype(jnp.bfloat16).reshape(1, rows, width)
    part_c = part_c.astype(jnp.bfloat16).reshape(1, rows, width)
    got_a, got_c = (
        lax.all_to_all(part_a, "ctx", split_axis=1, concat_axis=0, tiled=True),
        lax.all_to_all(part_c, "ctx", split_axis=1, concat_axis=0, tiled=True),
    )
    got_peak, got_total, got_bend = (
        lax.all_to_all(peak.T[None], "ctx", split_axis=1, concat_axis=0, tiled=True),
        lax.all_to_all(total.T[None], "ctx", split_axis=1, concat_axis=0, tiled=True),
        lax.all_to_all(bend.T[None], "ctx", split_axis=1, concat_axis=0, tiled=True),
    )
    top = jnp.max(got_peak, axis=0)
    weights = jnp.exp(got_peak - top[None])
    norm = jnp.sum(weights * got_total, axis=0)
    bent = jnp.sum(weights * got_bend, axis=0)
    numer = jnp.sum(
        weights[..., None] * got_a.astype(jnp.float32).reshape(n_ctx, q_dev, HEADS, HDIM), axis=0
    )
    tang = jnp.sum(
        weights[..., None] * got_c.astype(jnp.float32).reshape(n_ctx, q_dev, HEADS, HDIM), axis=0
    )
    attended = numer / norm[..., None]
    attended_t = tang / norm[..., None] - (bent / norm)[..., None] * attended
    high = jnp.max(pair_index[0])
    low = jnp.min(pair_index[0])
    gap = (high + 1 - low).astype(jnp.float32) / time_grid
    out_b = attended.reshape(q_dev, width).astype(jnp.bfloat16)
    scaled_t = (gap * attended_t).reshape(q_dev, width).astype(jnp.bfloat16)
    back_dims = (((1,), (1,)), ((), ()))
    column_weight = lax.all_gather(out_weight, "dp", axis=0, tiled=True)
    out_rows, scaled_rows = (
        lax.all_gather(out_b, "ctx", axis=0, tiled=True),
        lax.all_gather(scaled_t, "ctx", axis=0, tiled=True),
    )
    vel_cols = lax.all_to_all(velocity, "ctx", split_axis=2, concat_axis=1, tiled=True)
    stacked = jnp.concatenate([out_rows, scaled_rows], axis=0)
    result = jnp.dot(stacked, column_weight, preferred_element_type=jnp.float32)
    err = result[:rows] - (vel_cols[0].astype(jnp.float32) - result[rows:])
    grad_u = err.astype(jnp.bfloat16)
    grad_o = lax.psum_scatter(
        lax.dot_general(
            grad_u, column_weight, back_dims, preferred_element_type=jnp.float32
        ).astype(jnp.bfloat16),
        "ctx",
        scatter_dimension=0,
        tiled=True,
    )
    go_all = lax.all_gather(grad_o[None], "ctx", axis=1, tiled=True)[0]
    grad_heads = grad_o.astype(jnp.float32).reshape(q_dev, HEADS, HDIM)
    delta = jnp.sum(grad_heads * attended, axis=-1)
    top_all, norm_all, delta_all = (
        lax.all_gather(top[None], "ctx", axis=1, tiled=True),
        lax.all_gather(norm[None], "ctx", axis=1, tiled=True),
        lax.all_gather(delta[None], "ctx", axis=1, tiled=True),
    )
    go_heads = go_all.reshape(rows, HEADS, HDIM)
    prob = jnp.exp(score - top_all[0].T[..., None]) / norm_all[0].T[..., None]
    prob_b = prob.astype(jnp.bfloat16)
    grad_values = jnp.einsum(
        "hqk,qhd->khd", prob_b, go_heads, preferred_element_type=jnp.float32
    ).astype(jnp.bfloat16)
    dprob = jnp.einsum("qhd,khd->hqk", go_heads, v_heads, preferred_element_type=jnp.float32)
    dscore = prob * (dprob - delta_all[0].T[..., None]) * scale
    ds_b = dscore.astype(jnp.bfloat16)
    grad_keys = jnp.einsum(
        "hqk,qhd->khd", ds_b, q_heads, preferred_element_type=jnp.float32
    ).astype(jnp.bfloat16)
    parts = jnp.einsum("hqk,khd->qhd", ds_b, k_heads, preferred_element_type=jnp.float32).reshape(
        rows, width
    )
    grad_queries = lax.psum_scatter(
        parts.astype(jnp.bfloat16), "ctx", scatter_dimension=0, tiled=True
    )
    return (
        grad_queries.reshape(1, q_dev, width),
        grad_keys.reshape(1, kv_dev, width),
        grad_values.reshape(1, kv_dev, width),
    )


def solution(mesh):
    return jax.shard_map(
        local,
        mesh=mesh,
        in_specs=(
            P("dp", "ctx", None),
            P("dp", "ctx", None),
            P("dp", "ctx", None),
            P("dp", "ctx", None),
            P("dp", "ctx", None),
            P("dp", "ctx", None),
            P("dp", "ctx", None),
            P("dp", "ctx"),
            P("dp", None),
        ),
        out_specs=(P("dp", "ctx", None), P("dp", "ctx", None), P("dp", "ctx", None)),
        check_vma=False,
    )
```

profile of v0, /device:TPU:24, one launch (start us, length us, event | category | flops | bytes accessed | tf_op | source)
XLA Modules:
  0.0 837.7 jit_solution(15752900138925042079)
XLA Ops:
  7.2 68.8 %all_gather.27 = bf16[1,128,2560]{2,1,0:T(8,128)(2,1)S(1)} all-gather(bf16[1,8,2560]{2,1,0:T(8,128)(2,1)} %param.9), channel_id=1, replica_groups=mesh['dp'=32,'ctx'=16] {'ctx'}, dimensions={1}, use_global_device_ids=true | all-gather | bytes 696320 | tf_op jit(solution)/shard_map/all_gather | solution.py:31
  76.8 55.8 %all_gather.31 = bf16[1,128,2560]{2,1,0:T(8,128)(2,1)S(1)} all-gather(bf16[1,8,2560]{2,1,0:T(8,128)(2,1)S(1)} %copy-done.6), channel_id=1, replica_groups=mesh['dp'=32,'ctx'=16] {'ctx'}, dimensions={1}, use_global_device_ids=true | all-gather | bytes 696320 | tf_op jit(solution)/shard_map/all_gather | solution.py:32
  144.0 6.5 all-to-all-start.4
  152.4 12.9 %all-to-all-done.4 = f32[16,1,160]{2,1,0:T(1,128)S(1)} async-done(((f32[16,1,160]{2,1,0:T(1,128)}), f32[16,1,160]{2,1,0:T(1,128)S(1)}, u32[]{:S(2)}, u32[]{:S(2)}) %all-to-all-start.4) | async-done | bytes 10272 | tf_op jit(solution)/shard_map/all_to_all | solution.py:64
  172.7 10.8 %all-to-all-done.1 = f32[16,1,160]{2,1,0:T(1,128)S(1)} async-done(((f32[16,1,160]{2,1,0:T(1,128)}), f32[16,1,160]{2,1,0:T(1,128)S(1)}, u32[]{:S(2)}, u32[]{:S(2)}) %all-to-all-start.1) | async-done | bytes 10272 | tf_op jit(solution)/shard_map/all_to_all | solution.py:63
  195.3 16.1 %reduce.6 = bf16[2560,8]{1,0:T(8,128)(2,1)} reduce(bf16[2560,1,8]{2,1,0:T(2,128)(2,1)} %bitcast.78, bf16[]{:T(256)} %broadcast.48), dimensions={1}, to_apply=%bitcast.49.reduce_sub_computation | reduce | bytes 81922
  213.7 14.3 %all-to-all-start.5 = ((bf16[16,2,640]{2,1,0:T(2,128)(2,1)}), bf16[16,2,640]{2,1,0:T(2,128)(2,1)S(1)}, u32[]{:S(2)}, u32[]{:S(2)}) async-start(bf16[16,2,640]{2,1,0:T(2,128)(2,1)} %reshape.148), calls=%async_computation.5 | async-start | bytes 81920 | tf_op jit(solution)/shard_map/all_to_all | solution.py:89
  234.9 6.4 reduce.14
  244.1 14.5 %all-to-all-start.3 = ((bf16[16,2,10240]{2,1,0:T(2,128)(2,1)}), bf16[16,2,10240]{2,1,0:T(2,128)(2,1)}, u32[]{:S(2)}, u32[]{:S(2)}) async-start(bf16[16,2,10240]{2,1,0:T(2,128)(2,1)} %reshape.158), calls=%async_computation.3 | async-start | bytes 1310720 | tf_op jit(solution)/shard_map/all_to_all | solution.py:59
  265.1 6.4 reduce.7
  274.4 10.5 %all-to-all-done.3 = bf16[16,2,10240]{2,1,0:T(2,128)(2,1)} async-done(((bf16[16,2,10240]{2,1,0:T(2,128)(2,1)}), bf16[16,2,10240]{2,1,0:T(2,128)(2,1)}, u32[]{:S(2)}, u32[]{:S(2)}) %all-to-all-start.3) | async-done | bytes 655392 | tf_op jit(solution)/shard_map/all_to_all | solution.py:59
  284.9 5.1 all-to-all-start.2
  292.0 48.1 %all_gather.33 = bf16[2560,160]{1,0:T(8,128)(2,1)} all-gather(bf16[80,160]{1,0:T(8,128)(2,1)S(1)} %copy-done.8), channel_id=1, replica_groups=mesh['dp'=32,'ctx'=16] {'dp'}, dimensions={0}, use_global_device_ids=true | all-gather | bytes 844800 | tf_op jit(solution)/shard_map/all_gather | solution.py:84
  345.6 3.9 bitcast_convert_fusion
  351.4 5.0 reshape.159
  356.4 5.0 reshape.157
  363.7 56.7 %all_gather.30 = bf16[128,2560]{1,0:T(8,128)(2,1)S(1)} all-gather(bf16[8,2560]{1,0:T(8,128)(2,1)S(1)} %get-tuple-element.10), channel_id=1, replica_groups=mesh['dp'=32,'ctx'=16] {'ctx'}, dimensions={0}, use_global_device_ids=true | all-gather | bytes 696320 | tf_op jit(solution)/shard_map/all_gather | solution.py:86
  420.4 52.8 %all_gather.32 = bf16[128,2560]{1,0:T(8,128)(2,1)S(1)} all-gather(bf16[8,2560]{1,0:T(8,128)(2,1)S(1)} %get-tuple-element.11), channel_id=1, replica_groups=mesh['dp'=32,'ctx'=16] {'ctx'}, dimensions={0}, use_global_device_ids=true | all-gather | bytes 696320 | tf_op jit(solution)/shard_map/all_gather | solution.py:87
  475.3 57.8 %all-gather.1 = f32[128,20]{1,0:T(8,128)S(1)} all-gather(f32[8,20]{1,0:T(8,128)S(1)} %get-tuple-element.5), channel_id=3, replica_groups=mesh['dp'=32,'ctx'=16] {'ctx'}, dimensions={0}, use_global_device_ids=true | all-gather | bytes 10880 | tf_op jit(solution)/shard_map/all_gather | solution.py:107
  533.2 45.6 %all-gather = f32[128,20]{1,0:T(8,128)S(1)} all-gather(f32[8,20]{1,0:T(8,128)S(1)} %reduce_max.28), channel_id=2, replica_groups=mesh['dp'=32,'ctx'=16] {'ctx'}, dimensions={0}, use_global_device_ids=true | all-gather | bytes 10880 | tf_op jit(solution)/shard_map/all_gather | solution.py:106
  578.9 27.7 %reduce-scatter.3.cloned.1.call-done = bf16[8,2560]{1,0:T(8,128)(2,1)} async-done(((bf16[128,2560]{1,0:T(8,128)(2,1)}), bf16[8,2560]{1,0:T(8,128)(2,1)}) %reduce-scatter.3.cloned.1.call-update) | async-done | bytes 40976 | tf_op jit(solution)/shard_map/reduce_scatter | solution.py:94
  606.6 61.6 %all-gather.2 = bf16[128,2560]{1,0:T(8,128)(2,1)} all-gather(bf16[8,2560]{1,0:T(8,128)(2,1)} %reduce-scatter.3.cloned.1.call-done), channel_id=4, replica_groups=mesh['dp'=32,'ctx'=16] {'ctx'}, dimensions={0}, use_global_device_ids=true | all-gather | bytes 696320 | tf_op jit(solution)/shard_map/all_gather | solution.py:102
  670.7 45.5 %all-gather.3 = f32[128,20]{1,0:T(8,128)S(1)} all-gather(f32[8,20]{1,0:T(8,128)S(1)} %copy.116), channel_id=5, replica_groups=mesh['dp'=32,'ctx'=16] {'ctx'}, dimensions={0}, use_global_device_ids=true | all-gather | bytes 10880 | tf_op jit(solution)/shard_map/all_gather | solution.py:108
  727.0 103.8 %reduce-scatter.5.cloned.1.call-done = bf16[8,2560]{1,0:T(8,128)(2,1)} async-done(((bf16[128,2560]{1,0:T(8,128)(2,1)}), bf16[8,2560]{1,0:T(8,128)(2,1)}) %reduce-scatter.5.cloned.1.call-update) | async-done | bytes 40976 | tf_op jit(solution)/shard_map/reduce_scatter | solution.py:125
  (94 shorter events, 80.4 us)
Async XLA Ops:
  7.2 69.2 %copy-start.4 = (bf16[1,144,2560]{2,1,0:T(8,128)(2,1)S(1)}, bf16[1,144,2560]{2,1,0:T(8,128)(2,1)}, u32[]{:S(2)}) copy-start(bf16[1,144,2560]{2,1,0:T(8,128)(2,1)} %param.11) | copy-start | bytes 2211844
  76.0 0.8 copy-start.6
  133.7 1.1 copy-start.3
  144.0 21.3 %all-to-all-start.4 = ((f32[16,1,160]{2,1,0:T(1,128)}), f32[16,1,160]{2,1,0:T(1,128)S(1)}, u32[]{:S(2)}, u32[]{:S(2)}) async-start(f32[16,1,160]{2,1,0:T(1,128)} %reshape.154), calls=%async_computation.4 | async-start | bytes 32768 | tf_op jit(solution)/shard_map/all_to_all | solution.py:64
  165.3 18.2 %all-to-all-start.1 = ((f32[16,1,160]{2,1,0:T(1,128)}), f32[16,1,160]{2,1,0:T(1,128)S(1)}, u32[]{:S(2)}, u32[]{:S(2)}) async-start(f32[16,1,160]{2,1,0:T(1,128)} %reshape.152), calls=%async_computation.1 | async-start | bytes 32768 | tf_op jit(solution)/shard_map/all_to_all | solution.py:63
  183.6 30.1 %all-to-all-start = ((f32[16,1,160]{2,1,0:T(1,128)}), f32[16,1,160]{2,1,0:T(1,128)S(1)}, u32[]{:S(2)}, u32[]{:S(2)}) async-start(f32[16,1,160]{2,1,0:T(1,128)} %reshape.150), calls=%async_computation | async-start | bytes 32768 | tf_op jit(solution)/shard_map/all_to_all | solution.py:62
  190.3 2.3 copy-start.7
  213.7 30.4 %all-to-all-start.5 = ((bf16[16,2,640]{2,1,0:T(2,128)(2,1)}), bf16[16,2,640]{2,1,0:T(2,128)(2,1)S(1)}, u32[]{:S(2)}, u32[]{:S(2)}) async-start(bf16[16,2,640]{2,1,0:T(2,128)(2,1)} %reshape.148), calls=%async_computation.5 | async-start | bytes 81920 | tf_op jit(solution)/shard_map/all_to_all | solution.py:89
  244.1 40.7 %all-to-all-start.3 = ((bf16[16,2,10240]{2,1,0:T(2,128)(2,1)}), bf16[16,2,10240]{2,1,0:T(2,128)(2,1)}, u32[]{:S(2)}, u32[]{:S(2)}) async-start(bf16[16,2,10240]{2,1,0:T(2,128)(2,1)} %reshape.158), calls=%async_computation.3 | async-start | bytes 1310720 | tf_op jit(solution)/shard_map/all_to_all | solution.py:59
  271.5 18.5 %copy-start.9 = (s32[1,2]{1,0:T(1,128)S(1)}, s32[1,2]{1,0:T(1,128)}, u32[]{:S(2)}) copy-start(s32[1,2]{1,0:T(1,128)} %param.17) | copy-start | bytes 28
  271.5 20.5 %copy-start.8 = (bf16[80,160]{1,0:T(8,128)(2,1)S(1)}, bf16[80,160]{1,0:T(8,128)(2,1)}, u32[]{:S(2)}) copy-start(bf16[80,160]{1,0:T(8,128)(2,1)} %param.16) | copy-start | bytes 76804
  284.9 71.5 %all-to-all-start.2 = ((bf16[16,2,10240]{2,1,0:T(2,128)(2,1)}), bf16[16,2,10240]{2,1,0:T(2,128)(2,1)}, u32[]{:S(2)}, u32[]{:S(2)}) async-start(bf16[16,2,10240]{2,1,0:T(2,128)(2,1)} %reshape.156), calls=%async_computation.2 | async-start | bytes 1310720 | tf_op jit(solution)/shard_map/all_to_all | solution.py:58
  290.0 316.7 %reduce-scatter.3.cloned.1.call-start = ((), (), s32[]{:S(2)}) async-start(), calls=%async_computation.8 | async-start | bytes 696320 | tf_op jit(solution)/shard_map/reduce_scatter | solution.py:94
  363.6 109.6 %copy-start = (bf16[2560,160]{1,0:T(8,128)(2,1)S(1)}, bf16[2560,160]{1,0:T(8,128)(2,1)}, u32[]{:S(2)}) copy-start(bf16[2560,160]{1,0:T(8,128)(2,1)} %all_gather.33) | copy-start | bytes 2457604
  475.3 355.6 %reduce-scatter.5.cloned.1.call-start = ((), (), s32[]{:S(2)}) async-start(), calls=%async_computation.9 | async-start | bytes 696320 | tf_op jit(solution)/shard_map/reduce_scatter | solution.py:125
  606.6 63.8 %copy-start.5 = (bf16[8,2560]{1,0:T(8,128)(2,1)S(1)}, bf16[8,2560]{1,0:T(8,128)(2,1)}, u32[]{:S(2)}) copy-start(bf16[8,2560]{1,0:T(8,128)(2,1)} %reduce-scatter.3.cloned.1.call-done) | copy-start | bytes 122884
  718.1 1.5 copy-start.1
  723.4 1.5 copy-start.2
Sparse Core Ops, SparseCore 0:
  475.4 131.1 reduce-scatter.2
  721.9 108.8 reduce-scatter.4
where the time goes:
time: 840 us; the launch traced here: 838 us
  blocking collectives  493 us (59%)
  waiting for transfers between devices  166 us (20%)
  local copies, waits for them, and re-layouts  53.6 us (6%)
  starting transfers between devices  47.6 us (6%)
  other arithmetic  40.5 us (5%)
  matrix products  21.7 us (3%)
  between operations  15.7 us (2%)
    reduce_scatter x1, waiting for transfers between devices, local(): lax.psum_scatter(parts.astype(jnp.bfloat16), 'ctx', scatter_dimension=0,...  104 us
    all_gather x1, blocking collectives, local(): lax.all_gather(queries, 'ctx', axis=1, tiled=True)  68.8 us
    all_gather x1, blocking collectives, local(): go_all = lax.all_gather(grad_o[None], 'ctx', axis=1, tiled=True)[0]  61.6 us
    all_gather x1, blocking collectives, local(): lax.all_gather(norm[None], 'ctx', axis=1, tiled=True)  57.8 us
    all_gather x1, blocking collectives, local(): lax.all_gather(out_b, 'ctx', axis=0, tiled=True)  56.7 us
    all_gather x1, blocking collectives, local(): lax.all_gather(query_tangent, 'ctx', axis=1, tiled=True)  55.8 us
    all_gather x1, blocking collectives, local(): lax.all_gather(scaled_t, 'ctx', axis=0, tiled=True)  52.8 us
    all_gather x1, blocking collectives, local(): column_weight = lax.all_gather(out_weight, 'dp', axis=0, tiled=True)  48.1 us
  transfers between devices with their start and end apart: 8, of which 5 were waited for; matrix products, arithmetic and copies ran while one was open for 10% of the time, Pallas kernels for 0%

commit v1 on v0

v1 whole, which is shorter than its diff:
```python
import jax
import jax.numpy as jnp
from jax import lax
from jax.experimental import pallas as pl
from jax.experimental.pallas import tpu as pltpu
from jax.sharding import PartitionSpec as P

HEADS = 20
HDIM = 128
GROUP = 5
PER_STEP = 2
COPIES = 112
time_grid = 15.0

F32 = jnp.float32
BF16 = jnp.bfloat16
MESH = pl.DeviceIdType.MESH
NT = (((1,), (1,)), ((), ()))
TN = (((0,), (0,)), ((), ()))
NN = (((1,), (0,)), ((), ()))


def mm(a, b, dims):
    return lax.dot_general(a, b, dims, preferred_element_type=F32)


class Net:
    def __init__(self, send, recv):
        self.send, self.recv, self.used, self.all = send, recv, 0, []

    def copy(self, src, dst, device):
        n = self.used
        self.used += 1
        c = pltpu.make_async_remote_copy(
            src_ref=src,
            dst_ref=dst,
            send_sem=self.send.at[n],
            recv_sem=self.recv.at[n],
            device_id=device,
            device_id_type=MESH,
        )
        c.start()
        self.all.append(c)
        return c


class Ring:
    def __init__(self, net, p, name, device):
        self.net, self.p = net, p
        self.right, self.left, self.far = [lax.rem(p + k, 4) for k in (1, 3, 2)]
        self.to = lambda q: {name: device(q)}

    def gather(self, buf, half):
        p, r, l = self.p, self.right, self.left
        at = lambda b, k: half(buf, b, k)
        go = lambda b, k, q: self.net.copy(at(b, k), at(b, k), self.to(q))
        a = go(p, 0, r)
        b = go(p, 1, l)
        c = go(p, 1, r)
        d = go(p, 0, l)

        def finish():
            a.wait_recv()
            e = go(l, 0, r)
            b.wait_recv()
            f = go(r, 1, l)
            for x in (c, d, e, f):
                x.wait_recv()

        return finish

    def scatter(self, buf, half, tmp, got_l, got_r, half1):
        p, r, l, o = self.p, self.right, self.left, self.far
        to_r, to_l = self.to(r), self.to(l)
        a = self.net.copy(half(buf, o, 0), tmp.at[0], to_r)
        b = self.net.copy(half(buf, o, 1), tmp.at[1], to_l)
        c = self.net.copy(half(buf, r, 1), half1(got_l, 1), to_r)
        d = self.net.copy(half(buf, l, 0), half1(got_r, 0), to_l)
        a.wait_recv()
        x = half(buf, r, 0)
        x[...] = (x[...].astype(F32) + tmp[0].astype(F32)).astype(BF16)
        e = self.net.copy(x, half1(got_l, 0), to_r)
        b.wait_recv()
        y = half(buf, l, 1)
        y[...] = (y[...].astype(F32) + tmp[1].astype(F32)).astype(BF16)
        f = self.net.copy(y, half1(got_r, 1), to_l)
        for w in (c, d, e, f):
            w.wait_recv()

    def exchange(self, src, dst):
        cs = [self.net.copy(src(q), dst, self.to(q)) for q in (self.right, self.left, self.far)]

        def finish():
            for c in cs:
                c.wait_recv()

        return finish


def rows_half(n):
    return lambda buf, b, k: buf.at[b, pl.ds(k * n, n)]


def rows_half1(n):
    return lambda buf, k: buf.at[pl.ds(k * n, n)]


def kernel(
    q_in, qt_in, vel_in, pair, k_hbm, v_hbm, kt_hbm, vt_hbm, w_hbm,
    gq_out, dk_hbm, dv_hbm,
    k_, v_, kt_, vt_, w_, dk_, dv_,
    qz, qx, vsrc, vz, vx, sc, sl,
    st, st_x, st_z, lm, dl, dl_x, dl_z, dm,
    s_c, s_tx, s_lx, s_rx, s_z, s_tz, s_lz, s_rz, s_full,
    g_c, g_tx, g_lx, g_rx, g_z, g_tz, g_lz, g_rz, g_full,
    a_c, a_tx, a_lx, a_rx, a_z, a_tz, a_lz, a_rz,
    load_sem, store_sem, send_sem, recv_sem,
):
    scale = HDIM ** (-0.5)
    ctx = lax.axis_index("ctx")
    dp = lax.axis_index("dp")
    x, zh = lax.div(ctx, 4), lax.rem(ctx, 4)
    zl, y, core = lax.div(dp, 8), lax.rem(lax.div(dp, 2), 4), lax.rem(dp, 2)

    net = Net(send_sem, recv_sem)
    ring_x = Ring(net, x, "ctx", lambda q: q * 4 + zh)
    ring_z = Ring(net, zh, "ctx", lambda q: x * 4 + q)
    ring_y = Ring(net, y, "dp", lambda q: zl * 8 + q * 2 + core)
    line_z = Ring(net, zl, "dp", lambda q: q * 8 + y * 2 + core)
    twin = {"dp": zl * 8 + y * 2 + (1 - core)}

    w_own = w_.at[zl, y, core]
    loads = [
        pltpu.make_async_copy(src, dst, load_sem.at[n])
        for n, (src, dst) in enumerate(
            [
                (w_hbm, w_own),
                (k_hbm.at[0], k_),
                (kt_hbm.at[0], kt_),
                (v_hbm.at[0], v_),
                (vt_hbm.at[0], vt_),
            ]
        )
    ]
    for c in loads:
        c.start()

    barrier = pltpu.get_barrier_semaphore()
    for ring in (ring_z, ring_x, ring_y, line_z):
        for pos in (ring.right, ring.left, ring.far):
            pl.semaphore_signal(barrier, inc=1, device_id=ring.to(pos), device_id_type=MESH)
    pl.semaphore_signal(barrier, inc=1, device_id=twin, device_id_type=MESH)

    qz[zh] = jnp.concatenate([q_in[0].astype(F32), qt_in[0].astype(F32)], axis=0).astype(BF16)
    vel = vel_in[0].astype(F32)
    for c in range(16):
        vsrc[c % 4, c // 4] = vel[:, c * 160 : (c + 1) * 160]
    high = jnp.maximum(pair[0, 0], pair[0, 1])
    low = jnp.minimum(pair[0, 0], pair[0, 1])
    gap = (high + 1 - low).astype(F32) / time_grid
    st[...] = jnp.ones_like(st)
    dl[...] = jnp.zeros_like(dl)
    pl.semaphore_wait(barrier, 13)

    q_done = ring_z.gather(qz, lambda buf, b, k: buf.at[b, :, pl.ds(k * 1280, 1280)])
    loads[0].wait()
    w_done = ring_y.exchange(lambda q: w_own, w_own)
    q_done()
    both = [qz[z].astype(F32) for z in range(4)]
    qx[x, 0] = jnp.concatenate([t[:8] for t in both], axis=0).astype(BF16)
    qx[x, 1] = jnp.concatenate([t[8:] for t in both], axis=0).astype(BF16)
    q_done = ring_x.gather(qx, lambda buf, b, k: buf.at[b, k])
    w_done()
    w_done = line_z.exchange(lambda q: w_.at[zl, :, core], w_.at[zl, :, core])
    vel_done = ring_z.exchange(lambda q: vsrc.at[q], vz.at[zh])
    vz[zh] = vsrc[zh]
    for c in loads[1:]:
        c.wait()
    q_done()

    def place(h):
        return (
            lax.div(h, GROUP),
            lax.rem(h, GROUP),
            pl.ds(pl.multiple_of(h * HDIM, HDIM), HDIM),
            pl.ds(pl.multiple_of(lax.rem(h, GROUP) * HDIM, HDIM), HDIM),
        )

    def over_heads(body):
        def step(n, carry):
            for k in range(PER_STEP):
                body(n * PER_STEP + k)
            return carry

        lax.fori_loop(0, HEADS // PER_STEP, step, 0)

    def scores(h):
        b, i, at, _ = place(h)
        q = qx[:, 0, :, at].reshape(128, HDIM)
        qt = qx[:, 1, :, at].reshape(128, HDIM)
        k = k_[:, at]
        score = mm(k, q, NT) * scale
        slope = (mm(k, qt, NT) + mm(kt_[:, at], q, NT)) * scale
        peak = jnp.max(score, axis=0, keepdims=True)
        expd = jnp.exp(score - peak)
        st[b, 0, pl.ds(i, 1), :] = peak
        st[b, 1, pl.ds(i, 1), :] = jnp.sum(expd, axis=0, keepdims=True)
        st[b, 2, pl.ds(i, 1), :] = jnp.sum(expd * slope, axis=0, keepdims=True)
        sc[h] = score
        sl[h] = slope

    over_heads(scores)

    def merged(parts):
        top = parts[0][0]
        for t in parts[1:]:
            top = jnp.maximum(top, t[0])
        w = [jnp.exp(t[0] - top) for t in parts]
        norm = sum(a * t[1] for a, t in zip(w, parts))
        bent = sum(a * t[2] for a, t in zip(w, parts))
        return top, norm, bent

    done = ring_x.exchange(lambda q: st.at[q], st_x.at[x])
    st_x[x] = st[x]
    done()
    top, norm, bent = merged([st_x[j] for j in range(4)])
    st_z[zh, 0] = top
    st_z[zh, 1] = norm
    st_z[zh, 2] = bent
    done = ring_z.exchange(lambda q: st_z.at[zh], st_z.at[zh])
    w_done()
    twin_copy = net.copy(w_.at[:, :, core], w_.at[:, :, core], twin)
    vel_done()
    vel_done = ring_x.exchange(lambda q: vz.at[:, q], vx.at[x])
    vx[x] = vz[:, x]
    done()
    top, norm, bent = merged([st_z[j] for j in range(4)])
    lm[x, 0] = top + jnp.log(norm)
    lm[x, 1] = bent / norm
    ring_x.exchange(lambda q: lm.at[x], lm.at[x])()

    def outputs(h):
        b, i, at, out = place(h)
        prob = jnp.exp(sc[h] - lm[b, 0, pl.ds(i, 1), :])
        mix = prob * (1.0 + gap * (sl[h] - lm[b, 1, pl.ds(i, 1), :]))
        sc[h] = prob
        part = mm(mix.astype(BF16), v_[:, at], TN) + mm((gap * prob).astype(BF16), vt_[:, at], TN)
        s_c[b, :, out] = part.astype(BF16)

    over_heads(outputs)

    def all_reduce(c, tx, lx, rx, z, tz, lz, rz, full):
        ring_x.scatter(c, rows_half(64), tx, lx, rx, rows_half1(64))
        t = c[x].astype(F32) + lx[...].astype(F32) + rx[...].astype(F32)
        z[...] = t.astype(BF16).reshape(4, 32, 640)
        ring_z.scatter(z, rows_half(16), tz, lz, rz, rows_half1(16))
        t = z[zh].astype(F32) + lz[...].astype(F32) + rz[...].astype(F32)
        full[x, zh] = t.astype(BF16)
        ring_z.gather(full, lambda buf, b, k: buf.at[x, b, pl.ds(16 * k, 16)])()
        ring_x.gather(full, lambda buf, b, k: buf.at[b, pl.ds(2 * k, 2)])()

    all_reduce(s_c, s_tx, s_lx, s_rx, s_z, s_tz, s_lz, s_rz, s_full)

    twin_copy.wait_recv()
    vel_done()
    u = -vx[...].reshape(128, 160)
    for b in range(4):
        u = u + mm(s_full[b].reshape(128, 640), w_[b].reshape(640, 160), NN)
    u = u.astype(BF16)
    for b in range(4):
        g_c[b] = mm(u, w_[b].reshape(640, 160), NT).astype(BF16)

    all_reduce(g_c, g_tx, g_lx, g_rx, g_z, g_tz, g_lz, g_rz, g_full)

    def values_back(h):
        b, i, at, out = place(h)
        go = g_full[b, :, :, out].reshape(128, HDIM)
        prob = sc[h]
        dprob = mm(v_[:, at], go, NT)
        dl[b, pl.ds(i, 1), :] = jnp.sum(prob * dprob, axis=0, keepdims=True)
        sl[h] = dprob
        dv_[:, at] = mm(prob.astype(BF16), go, NN).astype(BF16)

    over_heads(values_back)
    dv_store = pltpu.make_async_copy(dv_, dv_hbm.at[0], store_sem.at[0])
    dv_store.start()

    done = ring_x.exchange(lambda q: dl.at[q], dl_x.at[x])
    dl_x[x] = dl[x]
    done()
    dl_z[zh] = dl_x[0] + dl_x[1] + dl_x[2] + dl_x[3]
    ring_z.exchange(lambda q: dl_z.at[zh], dl_z.at[zh])()
    dm[x] = dl_z[0] + dl_z[1] + dl_z[2] + dl_z[3]
    ring_x.exchange(lambda q: dm.at[x], dm.at[x])()

    def keys_back(h):
        b, i, at, out = place(h)
        ds = (sc[h] * (sl[h] - dm[b, pl.ds(i, 1), :]) * scale).astype(BF16)
        dk_[:, at] = mm(ds, qx[:, 0, :, at].reshape(128, HDIM), NN).astype(BF16)
        a_c[:, :, at] = mm(ds, k_[:, at], TN).astype(BF16).reshape(4, 32, HDIM)

    over_heads(keys_back)
    dk_store = pltpu.make_async_copy(dk_, dk_hbm.at[0], store_sem.at[1])
    dk_store.start()

    ring_x.scatter(a_c, rows_half(16), a_tx, a_lx, a_rx, rows_half1(16))
    t = a_c[x].astype(F32) + a_lx[...].astype(F32) + a_rx[...].astype(F32)
    for z in range(4):
        r = t[8 * z : 8 * z + 8]
        a_z[z] = jnp.concatenate([r[:, :1280], r[:, 1280:]], axis=0).astype(BF16)
    cols = lambda buf, k: buf.at[:, pl.ds(640 * k, 640)]
    ring_z.scatter(
        a_z, lambda buf, b, k: buf.at[b, :, pl.ds(640 * k, 640)], a_tz, a_lz, a_rz, cols
    )
    t = a_z[zh].astype(F32) + a_lz[...].astype(F32) + a_rz[...].astype(F32)
    gq_out[0] = jnp.concatenate([t[:8], t[8:]], axis=1).astype(BF16)

    for c in net.all:
        c.wait_send()
    dv_store.wait()
    dk_store.wait()


def vm(*shape, dtype=BF16):
    return pltpu.VMEM(shape, dtype)


def reduce_scratch():
    return [
        vm(4, 128, 640), vm(2, 64, 640), vm(128, 640), vm(128, 640),
        vm(4, 32, 640), vm(2, 16, 640), vm(32, 640), vm(32, 640), vm(4, 4, 32, 640),
    ]


def local(queries, query_tangent, keys, values, key_tangent, value_tangent, velocity, out_weight, pair_index):
    vmem = pl.BlockSpec(memory_space=pltpu.VMEM)
    smem = pl.BlockSpec(memory_space=pltpu.SMEM)
    hbm = pl.BlockSpec(memory_space=pl.ANY)
    return tuple(
        pl.pallas_call(
            kernel,
            out_shape=[
                jax.ShapeDtypeStruct((1, 8, 2560), BF16),
                jax.ShapeDtypeStruct((1, 144, 2560), BF16),
                jax.ShapeDtypeStruct((1, 144, 2560), BF16),
            ],
            in_specs=[vmem, vmem, vmem, smem] + [hbm] * 5,
            out_specs=[vmem, hbm, hbm],
            scratch_shapes=[
                *[vm(144, 2560)] * 4,
                vm(4, 4, 2, 80, 160),
                *[vm(144, 2560)] * 2,
                vm(4, 16, 2560),
                vm(4, 2, 32, 2560),
                *[vm(4, 4, 8, 160, dtype=F32)] * 3,
                *[vm(HEADS, 144, 128, dtype=F32)] * 2,
                *[vm(4, 3, 8, 128, dtype=F32)] * 3,
                vm(4, 2, 8, 128, dtype=F32),
                *[vm(4, 8, 128, dtype=F32)] * 4,
                *reduce_scratch(),
                *reduce_scratch(),
                vm(4, 32, 2560), vm(2, 16, 2560), vm(32, 2560), vm(32, 2560),
                vm(4, 16, 1280), vm(2, 16, 640), vm(16, 1280), vm(16, 1280),
                pltpu.SemaphoreType.DMA((5,)),
                pltpu.SemaphoreType.DMA((2,)),
                pltpu.SemaphoreType.DMA((COPIES,)),
                pltpu.SemaphoreType.DMA((COPIES,)),
            ],
            compiler_params=pltpu.CompilerParams(
                collective_id=0, has_side_effects=True, vmem_limit_bytes=48 * 1024 * 1024
            ),
        )(
            queries, query_tangent, velocity, pair_index,
            keys, values, key_tangent, value_tangent, out_weight,
        )
    )


def solution(mesh):
    row = P("dp", "ctx", None)
    return jax.shard_map(
        local,
        mesh=mesh,
        in_specs=(row,) * 7 + (P("dp", "ctx"), P("dp", None)),
        out_specs=(row, row, row),
        check_vma=False,
    )
```

time: 840 us -> 190 us (0.23)
  blocking collectives: 493 us -> 0 us
  Pallas kernels: 0 us -> 175 us
  waiting for transfers between devices: 166 us -> 0 us
  starting transfers between devices: 47.6 us -> 0 us
  local copies, waits for them, and re-layouts: 53.6 us -> 10.6 us
  other arithmetic: 40.5 us -> 0 us
  matrix products: 21.7 us -> 0 us
  between operations: 15.7 us -> 0.66 us
    all_gather x9 -> x0, blocking collectives: 493 us -> none  [the longest x1 68.8 us: local(): lax.all_gather(queries, 'ctx', axis=1, tiled=True)]
    pallas_call x0 -> x1, Pallas kernels: none -> 175 us  [local(): pl.pallas_call(kernel, out_shape=[jax.ShapeDtypeStruct((1, 8, 2560), BF16...]
    reduce_scatter x2 -> x0, waiting for transfers between devices: 132 us -> none  [the longest x1 104 us: local(): lax.psum_scatter(parts.astype(jnp.bfloat16), 'ctx', scatter_dimension=0,...]
    all_to_all x6 -> x0, starting transfers between devices: 47.5 us -> none  [the longest x1 14.5 us: local(): lax.all_to_all(part_c, 'ctx', split_axis=1, concat_axis=0, tiled=True)]
    all_to_all x6 -> x0, waiting for transfers between devices: 34.3 us -> none  [the longest x1 12.9 us: local(): lax.all_to_all(bend.T[None], 'ctx', split_axis=1, concat_axis=0, tiled=True)]
    unnamed x6 -> x0, other arithmetic: 31.3 us -> none
    dot_general x12 -> x0, matrix products: 21.7 us -> none  [the longest x1 3.11 us: local(): jnp.einsum('hqk,khd->qhd', expd_b, vt_heads, preferred_element_type=jnp.f...]
    unnamed x35 -> x21, local copies, waits for them, and re-layouts: 27.1 us -> 10.6 us
  transfers between devices with their start and end apart: 8 -> 0, of which waited for: 5 -> 0; matrix products, arithmetic and copies ran while one was open for 10% -> 0% of each run, Pallas kernels for 0% -> 0%
where the time goes in v1:
time: 190 us; the launch traced here: 186 us
  Pallas kernels  175 us (92%)
  local copies, waits for them, and re-layouts  10.6 us (6%)
    pallas_call x1, Pallas kernels, local(): pl.pallas_call(kernel, out_shape=[jax.ShapeDtypeStruct((1, 8, 2560), BF16...  175 us
    unnamed x21, local copies, waits for them, and re-layouts  10.6 us

profile of v1, /device:TPU:24, one launch (start us, length us, event | category | flops | bytes accessed | tf_op | source)
XLA Modules:
  0.0 186.2 jit_solution(17547383239577873540)
XLA Ops:
  0.6 0.0 copy-start
  0.6 1.1 copy-done
  1.8 0.0 copy-start.1
  1.8 1.1 copy-done.1
  2.9 0.0 copy-start.2
  2.9 1.1 copy-done.2
  4.0 0.0 copy-start.3
  4.0 1.1 copy-done.3
  5.1 0.0 copy-start.4
  5.1 0.8 copy-done.4
  5.9 0.0 copy-start.5
  5.9 0.8 copy-done.5
  6.7 0.0 copy-start.6
  6.7 0.8 copy-done.6
  7.4 0.0 copy-start.7
  7.4 0.8 copy-done.7
  8.2 0.0 copy-start.8
  8.2 0.7 copy-done.8
  8.9 175.0 %shard_map.112 = (bf16[1,8,2560]{2,1,0:T(8,128)(2,1)S(1)}, bf16[1,144,2560]{2,1,0:T(8,128)(2,1)S(1)}, bf16[1,144,2560]{2,1,0:T(8,128)(2,1)S(1)}) custom-call(bf16[1,8,2560]{2,1,0:T(8,128)(2,1)S(1)} %copy-done.4, bf16[1,8,2560]{2,1,0:T(8,128)(2,1)S(1)} %copy-done.5, bf16[1,8,2560]{2,1,0:T(8,128)(2,1)S(1)} %copy-done.6, s32[1,2]{1,0:T(1,128)S(1)} %copy-done.8, ...), custom_call_target="tpu_custom_call" | custom-call | tf_op jit(solution)/shard_map/pallas_call | solution.py:340
  183.8 0.6 copy.15
  184.5 0.9 copy.16
  185.3 0.9 copy.17
Async XLA Ops:
  0.6 1.1 copy-start
  1.8 1.1 copy-start.1
  2.9 1.1 copy-start.2
  4.0 1.1 copy-start.3
  5.1 0.8 copy-start.4
  5.9 0.8 copy-start.5
  6.7 0.8 copy-start.6
  7.4 0.8 copy-start.7
  8.2 0.7 copy-start.8
